TPU v7x, 32 devices: a whole 2x2x4 slice. The times are simulated.
32 devices in a mesh: groups: 2 (over y), rows: 16 (over z, x, core).
Axes of the slice: x: 2, y: 2, z: 4, core: 2. Of those that a mesh axis runs over, the one named last changes fastest.
Arguments:
- transition_tiles: bfloat16 [2048, 5, 128, 128], P(('groups', 'rows')), parts along dimension 0, may hold values from 0.049804688 to 1
- column_tiles: int32 [2048, 5], P(('groups', 'rows')), parts along dimension 0, may hold values from 0 to 1023, as said below
- schur_basis: bfloat16 [32, 262144], P(None, ('groups', 'rows')), parts along dimension 1, may hold values from -60 to 60
- membership_map: float32 [64, 32], P('groups'), parts along dimension 0, may hold values from -1 to 1
Outputs:
- memberships: float32 [32, 262144], P(None, ('groups', 'rows')), parts along dimension 1
There are 2 independent parts, one for each index of `groups`. A program takes and returns all parts, laid end to end along the dimension named above; each array names one. Nothing has to cross between parts.
Inputs may be any that keep to these rules, and one draw needn't show every extreme that they name: `column_tiles`: the 5 entries of row tile r are distinct column tiles, r itself among them, all within 64 of r; some row tile has one at distance exactly 64.
All inputs are finite; a program needn't handle non-finite values.
Results may differ from a plain program's by a relative error of at most 0.0045.
Values may be sent and summed in bfloat16 or wider, within the bound.
No kernel may reach another device: no remote copies, remote signals or barrier semaphores. Data moves between devices by JAX's collectives and lax.ppermute only.
A program may use at most 64 MiB of HBM per device.

v0:
```python
import jax
import jax.numpy as jnp
from jax import lax
from jax.sharding import PartitionSpec as P

PRODUCTS = 4


def padded_2(block, sides, width):
    for axis, dim in sides:
        count = lax.axis_size(axis)
        forward = [(i, i + 1) for i in range(count - 1)]
        backward = [(target, source) for source, target in forward]
        low = lax.ppermute(
            lax.slice_in_dim(block, block.shape[dim] - width, None, axis=dim), axis, forward
        )
        high = lax.ppermute(lax.slice_in_dim(block, 0, width, axis=dim), axis, backward)
        block = jnp.concatenate([low, block, high], axis=dim)
    return block


def tile_product(transition_tiles, local_index, row_total, padded):
    vector_count = padded.shape[0]
    tile_size = transition_tiles.shape[-1]
    blocks = padded.reshape(vector_count, -1, tile_size)
    picked = jnp.take(blocks, local_index, axis=1)
    summed = jnp.einsum(
        "rsij,vrsj->vri", transition_tiles, picked, preferred_element_type=jnp.float32
    )
    return (summed / row_total[None]).reshape(vector_count, -1)


def body(transition_tiles, column_tiles, schur_basis, membership_map):
    panel_tiles = transition_tiles.shape[0]
    tile_size = transition_tiles.shape[-1]
    shard_width = schur_basis.shape[1]
    state_count = shard_width * lax.axis_size("rows")
    own_first = lax.axis_index("rows") * panel_tiles
    first_tile = own_first - panel_tiles
    local_index = column_tiles - first_tile
    unit_vector = jnp.ones((tile_size,), jnp.bfloat16)
    row_total = jnp.einsum(
        "rsij,j->ri", transition_tiles, unit_vector, preferred_element_type=jnp.float32
    )
    padded = padded_2(schur_basis, (("rows", 1),), shard_width)
    result = tile_product(transition_tiles, local_index, row_total, padded)
    for step in range(PRODUCTS - 1):
        image = result.astype(jnp.bfloat16)
        padded_image = padded_2(image, (("rows", 1),), shard_width)
        result = tile_product(transition_tiles, local_index, row_total, padded_image)
    gram_local = (
        jnp.dot(
            result, result.T, precision=lax.Precision.HIGHEST, preferred_element_type=jnp.float32
        )
        / state_count
    )
    gram_total = lax.psum(gram_local, "rows")
    factor = jnp.linalg.cholesky(gram_total)
    basis_q = jax.scipy.linalg.solve_triangular(factor, result, lower=True)
    return jnp.dot(
        membership_map.T,
        basis_q,
        precision=lax.Precision.HIGHEST,
        preferred_element_type=jnp.float32,
    )


def solution(mesh):
    return jax.shard_map(
        body,
        mesh=mesh,
        in_specs=(
            P(("groups", "rows"), None, None, None),
            P(("groups", "rows"), None),
            P(None, ("groups", "rows")),
            P("groups", None),
        ),
        out_specs=P(None, ("groups", "rows")),
        check_vma=False,
    )
```

profile of v0, /device:TPU:0, one launch (start us, length us, event | category | flops | bytes accessed | tf_op | source)
XLA Modules:
  0.0 183.3 jit_solution(8848551696498775349)
XLA Ops:
  0.0 2.5 %collective-permute-start = (bf16[32,8192]{1,0:T(8,128)(2,1)}, bf16[32,8192]{1,0:T(8,128)(2,1)S(1)}, u32[]{:S(2)}, u32[]{:S(2)}) collective-permute-start(bf16[32,8192]{1,0:T(8,128)(2,1)} %param.8), channel_id=1, source_target_pairs={{0,1},{1,2},{2,3},{3,4},{4,5},{5,6},{6,7},{7,8},{8,9},{9,10},{10,1... | collective-permute-start | bytes 1572872 | tf_op jit(solution)/shard_map/ppermute | solution.py:14
  2.5 1.3 collective-permute-start.1
  3.8 6.6 %convert_reduce_fusion = bf16[64,128,128]{2,1,0:T(8,128)(2,1)S(1)} fusion(bf16[64,5,128,128]{3,2,1,0:T(8,128)(2,1)} %param.6), kind=kLoop, calls=%fused_computation.4 | loop fusion | flops 9437184 | bytes 12582912 | tf_op jit(solution)/shard_map/rsij,j->ri/reduce_sum | solution.py:42
  10.8 0.6 fusion.58
  11.5 1.3 copy_bitcast_fusion.3
  12.8 3.0 %gather_fusion = bf16[320,32,128]{2,1,0:T(8,128)(2,1)} fusion(bf16[32,192,128]{2,0,1:T(8,128)(2,1)S(1)} %copy_bitcast_fusion.3, s32[1024]{0:T(1024)S(1)} %pad_clamp_fusion), kind=kCustom, calls=%fused_computation.clone | custom fusion | bytes 5244160 | tf_op jit(solution)/shard_map/jit(_take)/gather | solution.py:26
  15.8 8.5 %fusion.52 = bf16[64,4,8,128]{3,2,1,0:T(8,128)(2,1)S(1)} fusion(bf16[64,5,128,128]{3,2,1,0:T(8,128)(2,1)} %param.6, bf16[64,5,32,128]{3,2,1,0:T(8,128)(2,1)} %bitcast.137, pred[64,5]{1,0:T(8,128)(4,1)S(1)} %copy.26, f32[64,128]{1,0:T(8,128)S(1)} %bitcast.149), kind=kOutput, calls=%fused_computation.50 | convolution fusion | flops 337379328 | bytes 13664576 | tf_op jit(solution)/shard_map/rsij,vrsj->vri/dot_general | solution.py:27
  24.4 1.3 collective-permute-start.3
  25.7 8.2 %collective-permute-start.2 = (bf16[32,8192]{1,0:T(8,128)(2,1)S(1)}, bf16[32,8192]{1,0:T(8,128)(2,1)S(1)}, u32[]{:S(2)}, u32[]{:S(2)}) collective-permute-start(bf16[32,8192]{1,0:T(8,128)(2,1)S(1)} %bitcast.141), channel_id=1, source_target_pairs={{0,1},{1,2},{2,3},{3,4},{4,5},{5,6},{6,7},{7,8},{8,9},{9,10},{10,1... | collective-permute-start | bytes 1572872 | tf_op jit(solution)/shard_map/ppermute | solution.py:14
  34.0 1.5 collective-permute-done.2
  35.4 0.3 copy_bitcast_fusion.2
  35.7 3.0 %gather_fusion.1 = bf16[320,32,128]{2,1,0:T(8,128)(2,1)} fusion(bf16[32,192,128]{2,0,1:T(8,128)(2,1)S(1)} %copy_bitcast_fusion.2, s32[1024]{0:T(1024)S(1)} %pad_clamp_fusion), kind=kCustom, calls=%fused_computation.1.clone | custom fusion | bytes 5244160 | tf_op jit(solution)/shard_map/jit(_take)/gather | solution.py:26
  38.7 8.5 %fusion.47 = bf16[64,4,8,128]{3,2,1,0:T(8,128)(2,1)S(1)} fusion(bf16[64,5,128,128]{3,2,1,0:T(8,128)(2,1)} %param.6, bf16[64,5,32,128]{3,2,1,0:T(8,128)(2,1)} %bitcast.138, pred[64,5]{1,0:T(8,128)(4,1)S(1)} %copy.26, f32[64,128]{1,0:T(8,128)S(1)} %bitcast.150), kind=kOutput, calls=%fused_computation.49 | convolution fusion | flops 337379328 | bytes 13664576 | tf_op jit(solution)/shard_map/rsij,vrsj->vri/dot_general | solution.py:27
  47.3 1.3 collective-permute-start.5
  48.6 13.6 %collective-permute-start.4 = (bf16[32,8192]{1,0:T(8,128)(2,1)S(1)}, bf16[32,8192]{1,0:T(8,128)(2,1)S(1)}, u32[]{:S(2)}, u32[]{:S(2)}) collective-permute-start(bf16[32,8192]{1,0:T(8,128)(2,1)S(1)} %bitcast.144), channel_id=1, source_target_pairs={{0,1},{1,2},{2,3},{3,4},{4,5},{5,6},{6,7},{7,8},{8,9},{9,10},{10,1... | collective-permute-start | bytes 1572872 | tf_op jit(solution)/shard_map/ppermute | solution.py:14
  62.2 1.3 collective-permute-done.4
  63.5 0.3 copy_bitcast_fusion.1
  63.8 3.0 %gather_fusion.2 = bf16[320,32,128]{2,1,0:T(8,128)(2,1)} fusion(bf16[32,192,128]{2,0,1:T(8,128)(2,1)S(1)} %copy_bitcast_fusion.1, s32[1024]{0:T(1024)S(1)} %pad_clamp_fusion), kind=kCustom, calls=%fused_computation.2.clone | custom fusion | bytes 5244160 | tf_op jit(solution)/shard_map/jit(_take)/gather | solution.py:26
  66.8 8.5 %fusion.42 = bf16[64,4,8,128]{3,2,1,0:T(8,128)(2,1)S(1)} fusion(bf16[64,5,128,128]{3,2,1,0:T(8,128)(2,1)} %param.6, bf16[64,5,32,128]{3,2,1,0:T(8,128)(2,1)} %bitcast.139, pred[64,5]{1,0:T(8,128)(4,1)S(1)} %copy.26, f32[64,128]{1,0:T(8,128)S(1)} %bitcast.151), kind=kOutput, calls=%fused_computation.48 | convolution fusion | flops 337379328 | bytes 13664576 | tf_op jit(solution)/shard_map/rsij,vrsj->vri/dot_general | solution.py:27
  75.4 1.3 collective-permute-start.7
  76.7 10.6 %collective-permute-start.6 = (bf16[32,8192]{1,0:T(8,128)(2,1)S(1)}, bf16[32,8192]{1,0:T(8,128)(2,1)S(1)}, u32[]{:S(2)}, u32[]{:S(2)}) collective-permute-start(bf16[32,8192]{1,0:T(8,128)(2,1)S(1)} %bitcast.147), channel_id=1, source_target_pairs={{0,1},{1,2},{2,3},{3,4},{4,5},{5,6},{6,7},{7,8},{8,9},{9,10},{10,1... | collective-permute-start | bytes 1572872 | tf_op jit(solution)/shard_map/ppermute | solution.py:14
  87.3 1.5 collective-permute-done.6
  89.1 3.0 %gather_fusion.3 = bf16[320,32,128]{2,1,0:T(8,128)(2,1)} fusion(bf16[32,192,128]{2,0,1:T(8,128)(2,1)S(1)} %copy_bitcast_fusion, s32[1024]{0:T(1024)S(1)} %pad_clamp_fusion), kind=kCustom, calls=%fused_computation.3.clone | custom fusion | bytes 5244160 | tf_op jit(solution)/shard_map/jit(_take)/gather | solution.py:26
  92.1 8.4 %fusion.37 = f32[64,32,128]{2,1,0:T(8,128)S(1)} fusion(bf16[64,5,128,128]{3,2,1,0:T(8,128)(2,1)} %param.6, bf16[64,5,32,128]{3,2,1,0:T(8,128)(2,1)} %bitcast.136, pred[64,5]{1,0:T(8,128)(4,1)S(1)} %copy.26, f32[64,128]{1,0:T(8,128)S(1)} %bitcast.152), kind=kOutput, calls=%fused_computation.47 | convolution fusion | flops 337117184 | bytes 14188864 | tf_op jit(solution)/shard_map/rsij,vrsj->vri/dot_general | solution.py:27
  100.6 1.0 fusion.32
  101.5 71.9 %psum.7 = f32[32,32]{0,1:T(8,128)S(1)} all-reduce(f32[32,32]{0,1:T(8,128)S(1)} %fusion.32), channel_id=1, replica_groups=mesh['groups'=2,'rows'=16] {'rows'}, use_global_device_ids=true, to_apply=%region_1.0 | all-reduce | flops 1024 | bytes 8192 | tf_op jit(solution)/shard_map/psum | solution.py:57
  173.6 2.9 %cholesky.16 = f32[32,32]{1,0:T(8,128)S(1)} custom-call(f32[32,32]{1,0:T(8,128)S(1)} %fusion.57), custom_call_target="Cholesky" | custom-call | tf_op jit(solution)/shard_map/jit(cholesky)/cholesky | solution.py:58
  176.5 0.6 compare_reduce_fusion
  177.1 0.7 fusion.55
  177.8 2.4 %custom-call.7 = f32[1,32,32]{1,2,0:T(8,128)S(1)} custom-call(f32[1,32,32]{2,1,0:T(8,128)S(1)} %fusion.55), custom_call_target="InvertDiagBlocksLowerTriangular" | custom-call | tf_op jit(solution)/shard_map/jit(_solve_triangular)/triangular_solve | solution.py:59
  180.2 1.1 fusion.33
  181.3 2.0 %convolution_bitcast_fusion = f32[32,8192]{1,0:T(8,128)} fusion(f32[32,8192]{1,0:T(8,128)S(1)} %fusion.33, f32[32,32]{1,0:T(8,128)S(1)} %copy-done), kind=kOutput, calls=%fused_computation.5 | convolution fusion | flops 100663296 | bytes 2101248 | tf_op jit(solution)/shard_map/dot_general | solution.py:60
  (23 shorter events, 1.1 us)
Async XLA Ops:
  0.0 181.3 %copy-start = (f32[32,32]{1,0:T(8,128)S(1)}, f32[32,32]{1,0:T(8,128)}, u32[]{:S(2)}) copy-start(f32[32,32]{1,0:T(8,128)} %param.9) | copy-start | bytes 12292
  0.0 11.5 %collective-permute-start = (bf16[32,8192]{1,0:T(8,128)(2,1)}, bf16[32,8192]{1,0:T(8,128)(2,1)S(1)}, u32[]{:S(2)}, u32[]{:S(2)}) collective-permute-start(bf16[32,8192]{1,0:T(8,128)(2,1)} %param.8), channel_id=1, source_target_pairs={{0,1},{1,2},{2,3},{3,4},{4,5},{5,6},{6,7},{7,8},{8,9},{9,10},{10,1... | collective-permute-start | bytes 1572872 | tf_op jit(solution)/shard_map/ppermute | solution.py:14
  2.5 8.9 %collective-permute-start.1 = (bf16[32,8192]{1,0:T(8,128)(2,1)}, bf16[32,8192]{1,0:T(8,128)(2,1)}, u32[]{:S(2)}, u32[]{:S(2)}) collective-permute-start(bf16[32,8192]{1,0:T(8,128)(2,1)} %param.8), channel_id=1, source_target_pairs={{1,0},{2,1},{3,2},{4,3},{5,4},{6,5},{7,6},{8,7},{9,8},{10,9},{11,1... | collective-permute-start | bytes 1572872 | tf_op jit(solution)/shard_map/ppermute | solution.py:17
  3.8 6.6 %copy-start.2 = (s32[64,5]{0,1:T(8,128)S(1)}, s32[64,5]{0,1:T(8,128)}, u32[]{:S(2)}) copy-start(s32[64,5]{0,1:T(8,128)} %param.7) | copy-start | bytes 3844
  3.8 7.6 %copy-start.1 = (bf16[32,8192]{1,0:T(8,128)(2,1)S(1)}, bf16[32,8192]{1,0:T(8,128)(2,1)}, u32[]{:S(2)}) copy-start(bf16[32,8192]{1,0:T(8,128)(2,1)} %param.8) | copy-start | bytes 1572868
  24.4 9.5 %collective-permute-start.3 = (bf16[32,8192]{1,0:T(8,128)(2,1)S(1)}, bf16[32,8192]{1,0:T(8,128)(2,1)S(1)}, u32[]{:S(2)}, u32[]{:S(2)}) collective-permute-start(bf16[32,8192]{1,0:T(8,128)(2,1)S(1)} %bitcast.140), channel_id=1, source_target_pairs={{1,0},{2,1},{3,2},{4,3},{5,4},{6,5},{7,6},{8,7},{9,8},{10,9},{11,1... | collective-permute-start | bytes 1572872 | tf_op jit(solution)/shard_map/ppermute | solution.py:17
  25.7 9.7 %collective-permute-start.2 = (bf16[32,8192]{1,0:T(8,128)(2,1)S(1)}, bf16[32,8192]{1,0:T(8,128)(2,1)S(1)}, u32[]{:S(2)}, u32[]{:S(2)}) collective-permute-start(bf16[32,8192]{1,0:T(8,128)(2,1)S(1)} %bitcast.141), channel_id=1, source_target_pairs={{0,1},{1,2},{2,3},{3,4},{4,5},{5,6},{6,7},{7,8},{8,9},{9,10},{10,1... | collective-permute-start | bytes 1572872 | tf_op jit(solution)/shard_map/ppermute | solution.py:14
  47.3 14.9 %collective-permute-start.5 = (bf16[32,8192]{1,0:T(8,128)(2,1)S(1)}, bf16[32,8192]{1,0:T(8,128)(2,1)S(1)}, u32[]{:S(2)}, u32[]{:S(2)}) collective-permute-start(bf16[32,8192]{1,0:T(8,128)(2,1)S(1)} %bitcast.143), channel_id=1, source_target_pairs={{1,0},{2,1},{3,2},{4,3},{5,4},{6,5},{7,6},{8,7},{9,8},{10,9},{11,1... | collective-permute-start | bytes 1572872 | tf_op jit(solution)/shard_map/ppermute | solution.py:17
  48.6 14.9 %collective-permute-start.4 = (bf16[32,8192]{1,0:T(8,128)(2,1)S(1)}, bf16[32,8192]{1,0:T(8,128)(2,1)S(1)}, u32[]{:S(2)}, u32[]{:S(2)}) collective-permute-start(bf16[32,8192]{1,0:T(8,128)(2,1)S(1)} %bitcast.144), channel_id=1, source_target_pairs={{0,1},{1,2},{2,3},{3,4},{4,5},{5,6},{6,7},{7,8},{8,9},{9,10},{10,1... | collective-permute-start | bytes 1572872 | tf_op jit(solution)/shard_map/ppermute | solution.py:14
  75.4 11.9 %collective-permute-start.7 = (bf16[32,8192]{1,0:T(8,128)(2,1)S(1)}, bf16[32,8192]{1,0:T(8,128)(2,1)S(1)}, u32[]{:S(2)}, u32[]{:S(2)}) collective-permute-start(bf16[32,8192]{1,0:T(8,128)(2,1)S(1)} %bitcast.146), channel_id=1, source_target_pairs={{1,0},{2,1},{3,2},{4,3},{5,4},{6,5},{7,6},{8,7},{9,8},{10,9},{11,1... | collective-permute-start | bytes 1572872 | tf_op jit(solution)/shard_map/ppermute | solution.py:17
  76.7 12.1 %collective-permute-start.6 = (bf16[32,8192]{1,0:T(8,128)(2,1)S(1)}, bf16[32,8192]{1,0:T(8,128)(2,1)S(1)}, u32[]{:S(2)}, u32[]{:S(2)}) collective-permute-start(bf16[32,8192]{1,0:T(8,128)(2,1)S(1)} %bitcast.147), channel_id=1, source_target_pairs={{0,1},{1,2},{2,3},{3,4},{4,5},{5,6},{6,7},{7,8},{8,9},{9,10},{10,1... | collective-permute-start | bytes 1572872 | tf_op jit(solution)/shard_map/ppermute | solution.py:14
where the time goes:
time: 184 us; the launch traced here: 183 us
  blocking collectives  71.9 us (39%)
  starting transfers between devices  40.1 us (22%)
  matrix products  38.6 us (21%)
  other arithmetic  15.4 us (8%)
  local copies, waits for them, and re-layouts  12.8 us (7%)
  waiting for transfers between devices  4.26 us (2%)
    psum x1, blocking collectives, body(): gram_total = lax.psum(gram_local, 'rows')  71.9 us
    ppermute x4, starting transfers between devices, padded_2(): lax.ppermute(lax.slice_in_dim(block, block.shape[dim] - width, None, axis...  34.9 us
    dot_general x4, matrix products, tile_product(): jnp.einsum('rsij,vrsj->vri', transition_tiles, picked, preferred_element_...  33.9 us
    gather x4, local copies, waits for them, and re-layouts, tile_product(): picked = jnp.take(blocks, local_index, axis=1)  12.1 us
    reduce_sum x1, other arithmetic, body(): jnp.einsum('rsij,j->ri', transition_tiles, unit_vector, preferred_element...  6.58 us
    ppermute x4, starting transfers between devices, padded_2(): lax.ppermute(lax.slice_in_dim(block, 0, width, axis=dim), axis, backward)  5.17 us
    ppermute x4, waiting for transfers between devices, padded_2(): lax.ppermute(lax.slice_in_dim(block, block.shape[dim] - width, None, axis...  4.25 us
  transfers between devices with their start and end apart: 8, of which 3 were waited for; matrix products, arithmetic and copies ran while one was open for 4% of the time, Pallas kernels for 0%

commit v1 on v0

--- a/solution.py
+++ b/solution.py
@@ -54,7 +54,8 @@
         )
         / state_count
     )
-    gram_total = lax.psum(gram_local, "rows")
+    quotas_build = lambda x0, mesh_name: jnp.sum(lax.all_gather(x0, mesh_name), 0)
+    gram_total = quotas_build(gram_local, "rows")
     factor = jnp.linalg.cholesky(gram_total)
     basis_q = jax.scipy.linalg.solve_triangular(factor, result, lower=True)
     return jnp.dot(

time: 184 us -> 147 us (0.80)
  blocking collectives: 71.9 us -> 35.3 us
    psum x1 -> x0, blocking collectives: 71.9 us -> none  [body(): gram_total = lax.psum(gram_local, 'rows')]
    all_gather x0 -> x1, blocking collectives: none -> 35.3 us  [body(): lax.all_gather(x0, mesh_name)]
  transfers between devices with their start and end apart: 8 -> 8, of which waited for: 3 -> 3; matrix products, arithmetic and copies ran while one was open for 4% -> 5% of each run, Pallas kernels for 0% -> 0%
where the time goes in v1:
time: 147 us
  starting transfers between devices  40.1 us (27%)
  matrix products  38.6 us (26%)
  blocking collectives  35.3 us (24%)
  other arithmetic  15.4 us (10%)
  local copies, waits for them, and re-layouts  12.8 us (9%)
  waiting for transfers between devices  4.26 us (3%)
    all_gather x1, blocking collectives, body(): lax.all_gather(x0, mesh_name)  35.3 us
    ppermute x4, starting transfers between devices, padded_2(): lax.ppermute(lax.slice_in_dim(block, block.shape[dim] - width, None, axis...  34.9 us
    dot_general x4, matrix products, tile_product(): jnp.einsum('rsij,vrsj->vri', transition_tiles, picked, preferred_element_...  33.9 us
    gather x4, local copies, waits for them, and re-layouts, tile_product(): picked = jnp.take(blocks, local_index, axis=1)  12.1 us
    reduce_sum x1, other arithmetic, body(): jnp.einsum('rsij,j->ri', transition_tiles, unit_vector, preferred_element...  6.58 us
    ppermute x4, starting transfers between devices, padded_2(): lax.ppermute(lax.slice_in_dim(block, 0, width, axis=dim), axis, backward)  5.17 us
    ppermute x4, waiting for transfers between devices, padded_2(): lax.ppermute(lax.slice_in_dim(block, block.shape[dim] - width, None, axis...  4.25 us
    another operation x3, other arithmetic, body(): factor = jnp.linalg.cholesky(gram_total)  3.59 us
  transfers between devices with their start and end apart: 8, of which 3 were waited for; matrix products, arithmetic and copies ran while one was open for 5% of the time, Pallas kernels for 0%

profile of v1, /device:TPU:0, one launch (start us, length us, event | category | flops | bytes accessed | tf_op | source)
XLA Modules:
  0.0 146.7 jit_solution(14275544095782436803)
XLA Ops:
  0.0 2.5 %collective-permute-start = (bf16[32,8192]{1,0:T(8,128)(2,1)}, bf16[32,8192]{1,0:T(8,128)(2,1)S(1)}, u32[]{:S(2)}, u32[]{:S(2)}) collective-permute-start(bf16[32,8192]{1,0:T(8,128)(2,1)} %param.8), channel_id=1, source_target_pairs={{0,1},{1,2},{2,3},{3,4},{4,5},{5,6},{6,7},{7,8},{8,9},{9,10},{10,1... | collective-permute-start | bytes 1572872 | tf_op jit(solution)/shard_map/ppermute | solution.py:14
  2.5 1.3 collective-permute-start.1
  3.8 6.6 %convert_reduce_fusion = bf16[64,128,128]{2,1,0:T(8,128)(2,1)S(1)} fusion(bf16[64,5,128,128]{3,2,1,0:T(8,128)(2,1)} %param.6), kind=kLoop, calls=%fused_computation.4 | loop fusion | flops 9437184 | bytes 12582912 | tf_op jit(solution)/shard_map/rsij,j->ri/reduce_sum | solution.py:42
  10.8 0.6 fusion.58
  11.5 1.3 copy_bitcast_fusion.3
  12.8 3.0 %gather_fusion = bf16[320,32,128]{2,1,0:T(8,128)(2,1)} fusion(bf16[32,192,128]{2,0,1:T(8,128)(2,1)S(1)} %copy_bitcast_fusion.3, s32[1024]{0:T(1024)S(1)} %pad_clamp_fusion), kind=kCustom, calls=%fused_computation.clone | custom fusion | bytes 5244160 | tf_op jit(solution)/shard_map/jit(_take)/gather | solution.py:26
  15.8 8.5 %fusion.52 = bf16[64,4,8,128]{3,2,1,0:T(8,128)(2,1)S(1)} fusion(bf16[64,5,128,128]{3,2,1,0:T(8,128)(2,1)} %param.6, bf16[64,5,32,128]{3,2,1,0:T(8,128)(2,1)} %bitcast.138, pred[64,5]{1,0:T(8,128)(4,1)S(1)} %copy.41, f32[64,128]{1,0:T(8,128)S(1)} %bitcast.151), kind=kOutput, calls=%fused_computation.50 | convolution fusion | flops 337379328 | bytes 13664576 | tf_op jit(solution)/shard_map/rsij,vrsj->vri/dot_general | solution.py:27
  24.4 1.3 collective-permute-start.3
  25.7 8.2 %collective-permute-start.2 = (bf16[32,8192]{1,0:T(8,128)(2,1)S(1)}, bf16[32,8192]{1,0:T(8,128)(2,1)S(1)}, u32[]{:S(2)}, u32[]{:S(2)}) collective-permute-start(bf16[32,8192]{1,0:T(8,128)(2,1)S(1)} %bitcast.142), channel_id=1, source_target_pairs={{0,1},{1,2},{2,3},{3,4},{4,5},{5,6},{6,7},{7,8},{8,9},{9,10},{10,1... | collective-permute-start | bytes 1572872 | tf_op jit(solution)/shard_map/ppermute | solution.py:14
  34.0 1.5 %collective-permute-done.2 = bf16[32,8192]{1,0:T(8,128)(2,1)S(1)} collective-permute-done((bf16[32,8192]{1,0:T(8,128)(2,1)S(1)}, bf16[32,8192]{1,0:T(8,128)(2,1)S(1)}, u32[]{:S(2)}, u32[]{:S(2)}) %collective-permute-start.2) | collective-permute-done | bytes 524320 | tf_op jit(solution)/shard_map/ppermute | solution.py:14
  35.4 0.3 copy_bitcast_fusion.2
  35.7 3.0 %gather_fusion.1 = bf16[320,32,128]{2,1,0:T(8,128)(2,1)} fusion(bf16[32,192,128]{2,0,1:T(8,128)(2,1)S(1)} %copy_bitcast_fusion.2, s32[1024]{0:T(1024)S(1)} %pad_clamp_fusion), kind=kCustom, calls=%fused_computation.1.clone | custom fusion | bytes 5244160 | tf_op jit(solution)/shard_map/jit(_take)/gather | solution.py:26
  38.7 8.5 %fusion.47 = bf16[64,4,8,128]{3,2,1,0:T(8,128)(2,1)S(1)} fusion(bf16[64,5,128,128]{3,2,1,0:T(8,128)(2,1)} %param.6, bf16[64,5,32,128]{3,2,1,0:T(8,128)(2,1)} %bitcast.139, pred[64,5]{1,0:T(8,128)(4,1)S(1)} %copy.41, f32[64,128]{1,0:T(8,128)S(1)} %bitcast.152), kind=kOutput, calls=%fused_computation.49 | convolution fusion | flops 337379328 | bytes 13664576 | tf_op jit(solution)/shard_map/rsij,vrsj->vri/dot_general | solution.py:27
  47.3 1.3 collective-permute-start.5
  48.6 13.6 %collective-permute-start.4 = (bf16[32,8192]{1,0:T(8,128)(2,1)S(1)}, bf16[32,8192]{1,0:T(8,128)(2,1)S(1)}, u32[]{:S(2)}, u32[]{:S(2)}) collective-permute-start(bf16[32,8192]{1,0:T(8,128)(2,1)S(1)} %bitcast.145), channel_id=1, source_target_pairs={{0,1},{1,2},{2,3},{3,4},{4,5},{5,6},{6,7},{7,8},{8,9},{9,10},{10,1... | collective-permute-start | bytes 1572872 | tf_op jit(solution)/shard_map/ppermute | solution.py:14
  62.2 1.3 collective-permute-done.4
  63.5 0.3 copy_bitcast_fusion.1
  63.8 3.0 %gather_fusion.2 = bf16[320,32,128]{2,1,0:T(8,128)(2,1)} fusion(bf16[32,192,128]{2,0,1:T(8,128)(2,1)S(1)} %copy_bitcast_fusion.1, s32[1024]{0:T(1024)S(1)} %pad_clamp_fusion), kind=kCustom, calls=%fused_computation.2.clone | custom fusion | bytes 5244160 | tf_op jit(solution)/shard_map/jit(_take)/gather | solution.py:26
  66.8 8.5 %fusion.42 = bf16[64,4,8,128]{3,2,1,0:T(8,128)(2,1)S(1)} fusion(bf16[64,5,128,128]{3,2,1,0:T(8,128)(2,1)} %param.6, bf16[64,5,32,128]{3,2,1,0:T(8,128)(2,1)} %bitcast.140, pred[64,5]{1,0:T(8,128)(4,1)S(1)} %copy.41, f32[64,128]{1,0:T(8,128)S(1)} %bitcast.153), kind=kOutput, calls=%fused_computation.48 | convolution fusion | flops 337379328 | bytes 13664576 | tf_op jit(solution)/shard_map/rsij,vrsj->vri/dot_general | solution.py:27
  75.4 1.3 collective-permute-start.7
  76.7 10.6 %collective-permute-start.6 = (bf16[32,8192]{1,0:T(8,128)(2,1)S(1)}, bf16[32,8192]{1,0:T(8,128)(2,1)S(1)}, u32[]{:S(2)}, u32[]{:S(2)}) collective-permute-start(bf16[32,8192]{1,0:T(8,128)(2,1)S(1)} %bitcast.148), channel_id=1, source_target_pairs={{0,1},{1,2},{2,3},{3,4},{4,5},{5,6},{6,7},{7,8},{8,9},{9,10},{10,1... | collective-permute-start | bytes 1572872 | tf_op jit(solution)/shard_map/ppermute | solution.py:14
  87.3 1.5 %collective-permute-done.6 = bf16[32,8192]{1,0:T(8,128)(2,1)S(1)} collective-permute-done((bf16[32,8192]{1,0:T(8,128)(2,1)S(1)}, bf16[32,8192]{1,0:T(8,128)(2,1)S(1)}, u32[]{:S(2)}, u32[]{:S(2)}) %collective-permute-start.6) | collective-permute-done | bytes 524320 | tf_op jit(solution)/shard_map/ppermute | solution.py:14
  89.1 3.0 %gather_fusion.3 = bf16[320,32,128]{2,1,0:T(8,128)(2,1)} fusion(bf16[32,192,128]{2,0,1:T(8,128)(2,1)S(1)} %copy_bitcast_fusion, s32[1024]{0:T(1024)S(1)} %pad_clamp_fusion), kind=kCustom, calls=%fused_computation.3.clone | custom fusion | bytes 5244160 | tf_op jit(solution)/shard_map/jit(_take)/gather | solution.py:26
  92.1 8.4 %fusion.37 = f32[64,32,128]{2,1,0:T(8,128)S(1)} fusion(bf16[64,5,128,128]{3,2,1,0:T(8,128)(2,1)} %param.6, bf16[64,5,32,128]{3,2,1,0:T(8,128)(2,1)} %bitcast.137, pred[64,5]{1,0:T(8,128)(4,1)S(1)} %copy.41, f32[64,128]{1,0:T(8,128)S(1)} %bitcast.154), kind=kOutput, calls=%fused_computation.47 | convolution fusion | flops 337117184 | bytes 14188864 | tf_op jit(solution)/shard_map/rsij,vrsj->vri/dot_general | solution.py:27
  100.6 1.0 fusion.32
  101.5 35.3 %all-gather = f32[512,32]{1,0:T(8,128)S(1)} all-gather(f32[32,32]{1,0:T(8,128)S(1)} %fusion.32), channel_id=2, replica_groups=mesh['groups'=2,'rows'=16] {'rows'}, dimensions={0}, use_global_device_ids=true | all-gather | bytes 69632 | tf_op jit(solution)/shard_map/all_gather | solution.py:57
  137.0 2.9 %cholesky.16 = f32[32,32]{1,0:T(8,128)S(1)} custom-call(f32[32,32]{1,0:T(8,128)S(1)} %fusion.57), custom_call_target="Cholesky" | custom-call | tf_op jit(solution)/shard_map/jit(cholesky)/cholesky | solution.py:59
  139.9 0.6 compare_reduce_fusion
  140.6 0.7 fusion.55
  141.2 2.4 %custom-call.7 = f32[1,32,32]{1,2,0:T(8,128)S(1)} custom-call(f32[1,32,32]{2,1,0:T(8,128)S(1)} %fusion.55), custom_call_target="InvertDiagBlocksLowerTriangular" | custom-call | tf_op jit(solution)/shard_map/jit(_solve_triangular)/triangular_solve | solution.py:60
  143.6 1.1 fusion.33
  144.7 2.0 %convolution_bitcast_fusion = f32[32,8192]{1,0:T(8,128)} fusion(f32[32,8192]{1,0:T(8,128)S(1)} %fusion.33, f32[32,32]{1,0:T(8,128)S(1)} %copy-done), kind=kOutput, calls=%fused_computation.5 | convolution fusion | flops 100663296 | bytes 2101248 | tf_op jit(solution)/shard_map/dot_general | solution.py:61
  (24 shorter events, 1.1 us)
Async XLA Ops:
  0.0 144.7 %copy-start = (f32[32,32]{1,0:T(8,128)S(1)}, f32[32,32]{1,0:T(8,128)}, u32[]{:S(2)}) copy-start(f32[32,32]{1,0:T(8,128)} %param.9) | copy-start | bytes 12292
  0.0 11.5 %collective-permute-start = (bf16[32,8192]{1,0:T(8,128)(2,1)}, bf16[32,8192]{1,0:T(8,128)(2,1)S(1)}, u32[]{:S(2)}, u32[]{:S(2)}) collective-permute-start(bf16[32,8192]{1,0:T(8,128)(2,1)} %param.8), channel_id=1, source_target_pairs={{0,1},{1,2},{2,3},{3,4},{4,5},{5,6},{6,7},{7,8},{8,9},{9,10},{10,1... | collective-permute-start | bytes 1572872 | tf_op jit(solution)/shard_map/ppermute | solution.py:14
  2.5 8.9 %collective-permute-start.1 = (bf16[32,8192]{1,0:T(8,128)(2,1)}, bf16[32,8192]{1,0:T(8,128)(2,1)}, u32[]{:S(2)}, u32[]{:S(2)}) collective-permute-start(bf16[32,8192]{1,0:T(8,128)(2,1)} %param.8), channel_id=1, source_target_pairs={{1,0},{2,1},{3,2},{4,3},{5,4},{6,5},{7,6},{8,7},{9,8},{10,9},{11,1... | collective-permute-start | bytes 1572872 | tf_op jit(solution)/shard_map/ppermute | solution.py:17
  3.8 6.6 %copy-start.2 = (s32[64,5]{0,1:T(8,128)S(1)}, s32[64,5]{0,1:T(8,128)}, u32[]{:S(2)}) copy-start(s32[64,5]{0,1:T(8,128)} %param.7) | copy-start | bytes 3844
  3.8 7.6 %copy-start.1 = (bf16[32,8192]{1,0:T(8,128)(2,1)S(1)}, bf16[32,8192]{1,0:T(8,128)(2,1)}, u32[]{:S(2)}) copy-start(bf16[32,8192]{1,0:T(8,128)(2,1)} %param.8) | copy-start | bytes 1572868
  24.4 9.5 %collective-permute-start.3 = (bf16[32,8192]{1,0:T(8,128)(2,1)S(1)}, bf16[32,8192]{1,0:T(8,128)(2,1)S(1)}, u32[]{:S(2)}, u32[]{:S(2)}) collective-permute-start(bf16[32,8192]{1,0:T(8,128)(2,1)S(1)} %bitcast.141), channel_id=1, source_target_pairs={{1,0},{2,1},{3,2},{4,3},{5,4},{6,5},{7,6},{8,7},{9,8},{10,9},{11,1... | collective-permute-start | bytes 1572872 | tf_op jit(solution)/shard_map/ppermute | solution.py:17
  25.7 9.7 %collective-permute-start.2 = (bf16[32,8192]{1,0:T(8,128)(2,1)S(1)}, bf16[32,8192]{1,0:T(8,128)(2,1)S(1)}, u32[]{:S(2)}, u32[]{:S(2)}) collective-permute-start(bf16[32,8192]{1,0:T(8,128)(2,1)S(1)} %bitcast.142), channel_id=1, source_target_pairs={{0,1},{1,2},{2,3},{3,4},{4,5},{5,6},{6,7},{7,8},{8,9},{9,10},{10,1... | collective-permute-start | bytes 1572872 | tf_op jit(solution)/shard_map/ppermute | solution.py:14
  47.3 14.9 %collective-permute-start.5 = (bf16[32,8192]{1,0:T(8,128)(2,1)S(1)}, bf16[32,8192]{1,0:T(8,128)(2,1)S(1)}, u32[]{:S(2)}, u32[]{:S(2)}) collective-permute-start(bf16[32,8192]{1,0:T(8,128)(2,1)S(1)} %bitcast.144), channel_id=1, source_target_pairs={{1,0},{2,1},{3,2},{4,3},{5,4},{6,5},{7,6},{8,7},{9,8},{10,9},{11,1... | collective-permute-start | bytes 1572872 | tf_op jit(solution)/shard_map/ppermute | solution.py:17
  48.6 14.9 %collective-permute-start.4 = (bf16[32,8192]{1,0:T(8,128)(2,1)S(1)}, bf16[32,8192]{1,0:T(8,128)(2,1)S(1)}, u32[]{:S(2)}, u32[]{:S(2)}) collective-permute-start(bf16[32,8192]{1,0:T(8,128)(2,1)S(1)} %bitcast.145), channel_id=1, source_target_pairs={{0,1},{1,2},{2,3},{3,4},{4,5},{5,6},{6,7},{7,8},{8,9},{9,10},{10,1... | collective-permute-start | bytes 1572872 | tf_op jit(solution)/shard_map/ppermute | solution.py:14
  75.4 11.9 %collective-permute-start.7 = (bf16[32,8192]{1,0:T(8,128)(2,1)S(1)}, bf16[32,8192]{1,0:T(8,128)(2,1)S(1)}, u32[]{:S(2)}, u32[]{:S(2)}) collective-permute-start(bf16[32,8192]{1,0:T(8,128)(2,1)S(1)} %bitcast.147), channel_id=1, source_target_pairs={{1,0},{2,1},{3,2},{4,3},{5,4},{6,5},{7,6},{8,7},{9,8},{10,9},{11,1... | collective-permute-start | bytes 1572872 | tf_op jit(solution)/shard_map/ppermute | solution.py:17
  76.7 12.1 %collective-permute-start.6 = (bf16[32,8192]{1,0:T(8,128)(2,1)S(1)}, bf16[32,8192]{1,0:T(8,128)(2,1)S(1)}, u32[]{:S(2)}, u32[]{:S(2)}) collective-permute-start(bf16[32,8192]{1,0:T(8,128)(2,1)S(1)} %bitcast.148), channel_id=1, source_target_pairs={{0,1},{1,2},{2,3},{3,4},{4,5},{5,6},{6,7},{7,8},{8,9},{9,10},{10,1... | collective-permute-start | bytes 1572872 | tf_op jit(solution)/shard_map/ppermute | solution.py:14
